TPU v7x, 512 devices: a whole 4x8x8 slice. The times are simulated.
512 devices in a mesh: blk: 64 (over y_lo, z, core), grp: 8 (over x, y_hi).
Axes of the slice: x: 4, y: 8 (y_hi: 2, y_lo: 4; y = y_hi * 4 + y_lo), z: 8, core: 2. Of those that a mesh axis runs over, the one named last changes fastest.
Arguments:
- embeddings: bfloat16 [262144, 512], P(('blk', 'grp')), may hold values from -6 to 6
- frame_weight: bfloat16 [262144], P(('blk', 'grp')), may hold values from 0.3984375 to 1.59375
- candidates: int32 [64, 8, 4, 8], P('blk', 'grp'), may hold values from 0 to 511, as said below
- owner: int32 [512], replicated, may hold values from 0 to 7, as said below
Outputs:
- best_score: float32 [262144], P(('blk', 'grp'))
- matches: bfloat16 [64, 8, 8, 2, 128, 128], P('blk', 'grp')
Inputs may be any that keep to these rules, and one draw needn't show every extreme that they name: `candidates`: offsets lie in 1..3, row and column blocks in 0..3, videos in 0..511. In each device's list at most 2 videos have one owner; for every blk index some owner gets exactly 2 from every grp device of it. `owner`: every partition owns exactly 64 videos.
All inputs are finite; a program needn't handle non-finite values.
Results may differ from a plain program's by a relative error of at most 0.001.
Values may be sent and summed in bfloat16 or wider, within the bound.
A program may use at most 64 MiB of HBM per device.

v0:
```python
import jax
import jax.numpy as jnp
from jax import lax
from jax.sharding import PartitionSpec as P

D = 512
ROT = 3
PIECE = 128
CAP = 2


def from_behind(value, axis, steps):
    count = lax.axis_size(axis)
    pairs = [(source, (source + steps) % count) for source in range(count)]
    return lax.ppermute(value, axis, pairs)


def smooth_tile(tile_scores, row_weight, col_weight):
    weight_pair = 0.25 * row_weight[:, None] * col_weight[None, :]
    for sweep_index in range(3):
        padded = jnp.pad(tile_scores, 1)
        tile_scores = tile_scores + weight_pair * (padded[:-2, :-2] + padded[2:, 2:])
    return tile_scores


def select_pieces(tile_scores, row_hot, col_hot):
    frames_here = tile_scores.shape[0]
    blocks = frames_here // PIECE
    count = row_hot.shape[0]
    picked_rows = jnp.einsum(
        "nr,rpx->npx",
        row_hot,
        tile_scores.reshape(blocks, PIECE, frames_here),
        precision=lax.Precision.HIGHEST,
    )
    return jnp.einsum(
        "nc,npcq->npq",
        col_hot,
        picked_rows.reshape(count, PIECE, blocks, PIECE),
        precision=lax.Precision.HIGHEST,
    )


def body(embeddings, frame_weight, candidates, owner):
    frames_here = embeddings.shape[0]
    groups = lax.axis_size("grp")
    videos_all = owner.shape[0]
    count = candidates.shape[3]
    blocks = frames_here // PIECE
    scale_factor = D ** (-0.5)
    row_weight = frame_weight.astype(jnp.float32)
    listing = candidates.reshape(4, count)
    tile_index, row_block, col_block, video_ids = (listing[0], listing[1], listing[2], listing[3])
    block_range = jnp.arange(blocks, dtype=jnp.int32)
    col_hot = (col_block[:, None] == block_range[None, :]).astype(jnp.float32)
    best_score = jnp.full((frames_here,), -jnp.inf, jnp.float32)
    pieces = jnp.zeros((count, PIECE, PIECE), jnp.float32)
    visiting = (embeddings, frame_weight)
    for offset in range(1, ROT + 1):
        visiting = from_behind((visiting[0], visiting[1]), "blk", 1)
        tile_scores = (
            lax.dot_general(
                embeddings,
                visiting[0],
                (((1,), (1,)), ((), ())),
                preferred_element_type=jnp.float32,
            )
            * scale_factor
        )
        tile_scores = smooth_tile(tile_scores, row_weight, visiting[1].astype(jnp.float32))
        best_score = jnp.maximum(best_score, jnp.max(tile_scores, axis=1))
        row_hot = (
            (row_block[:, None] == block_range[None, :]) & (tile_index == offset)[:, None]
        ).astype(jnp.float32)
        pieces = pieces + select_pieces(tile_scores, row_hot, col_hot)
    pieces_low = pieces.astype(jnp.bfloat16)
    video_range = jnp.arange(videos_all, dtype=jnp.int32)
    destination = jnp.sum(
        jnp.where(video_ids[:, None] == video_range[None, :], owner[None, :], 0), axis=1
    )
    list_range = jnp.arange(count, dtype=jnp.int32)
    same_owner = (destination[:, None] == destination[None, :]) & (
        list_range[None, :] < list_range[:, None]
    )
    slot_rank = jnp.sum(same_owner.astype(jnp.int32), axis=1)
    dest_hot = (destination[:, None] == jnp.arange(groups, dtype=jnp.int32)[None, :]).astype(
        jnp.bfloat16
    )
    slot_hot = (slot_rank[:, None] == jnp.arange(CAP, dtype=jnp.int32)[None, :]).astype(
        jnp.bfloat16
    )
    bucket = jnp.einsum(
        "nd,nc,nxy->dcxy", dest_hot, slot_hot, pieces_low, preferred_element_type=jnp.float32
    ).astype(jnp.bfloat16)
    received = lax.all_to_all(bucket, "grp", split_axis=0, concat_axis=0, tiled=True)
    return (best_score, received.reshape(1, 1, groups, CAP, PIECE, PIECE))


def solution(mesh):
    return jax.shard_map(
        body,
        mesh=mesh,
        in_specs=(P(("blk", "grp"), None), P(("blk", "grp")), P("blk", "grp", None, None), P()),
        out_specs=(P(("blk", "grp")), P("blk", "grp", None, None, None, None)),
        check_vma=False,
    )
```

profile of v0, /device:TPU:2, one launch (start us, length us, event | category | flops | bytes accessed | tf_op | source)
XLA Modules:
  0.0 95.3 jit_solution(3615492539824217137)
XLA Ops:
  0.6 0.0 copy-start
  0.6 2.1 %collective-permute-start.1 = (bf16[512]{0:T(512)(128)(2,1)}, bf16[512]{0:T(512)(128)(2,1)S(1)}, u32[]{:S(2)}, u32[]{:S(2)}) collective-permute-start(bf16[512]{0:T(512)(128)(2,1)} %param.5), channel_id=1, source_target_pairs={{0,8},{8,16},{16,24},{24,32},{32,40},{40,48},{48,56},{56,64},{64,7... | collective-permute-start | bytes 3080 | tf_op jit(solution)/shard_map/ppermute | solution.py:15
  2.7 4.4 %collective-permute-start = (bf16[512,512]{1,0:T(8,128)(2,1)}, bf16[512,512]{1,0:T(8,128)(2,1)S(1)}, u32[]{:S(2)}, u32[]{:S(2)}) collective-permute-start(bf16[512,512]{1,0:T(8,128)(2,1)} %param.4), channel_id=1, source_target_pairs={{0,8},{8,16},{16,24},{24,32},{32,40},{40,48},{48,56},{56,64},{64,7... | collective-permute-start | bytes 1572872 | tf_op jit(solution)/shard_map/ppermute | solution.py:15
  7.1 0.7 convert_multiply_fusion
  7.8 0.8 slice_bitcast_fusion.2
  8.6 0.7 compare_bitcast_fusion.2
  9.3 0.9 select_reduce_fusion
  10.1 0.1 fusion.37
  10.2 5.4 %collective-permute-done.1 = bf16[512]{0:T(512)(128)(2,1)S(1)} collective-permute-done((bf16[512]{0:T(512)(128)(2,1)}, bf16[512]{0:T(512)(128)(2,1)S(1)}, u32[]{:S(2)}, u32[]{:S(2)}) %collective-permute-start.1) | collective-permute-done | bytes 1056 | tf_op jit(solution)/shard_map/ppermute | solution.py:15
  15.7 1.9 %collective-permute-start.3 = (bf16[512]{0:T(512)(128)(2,1)S(1)}, bf16[512]{0:T(512)(128)(2,1)S(1)}, u32[]{:S(2)}, u32[]{:S(2)}) collective-permute-start(bf16[512]{0:T(512)(128)(2,1)S(1)} %collective-permute-done.1), channel_id=1, source_target_pairs={{0,8},{8,16},{16,24},{24,32},{32,40},{40,48},{48,56},{56,64},{64,7... | collective-permute-start | bytes 3080 | tf_op jit(solution)/shard_map/ppermute | solution.py:15
  17.6 5.6 %collective-permute-done = bf16[512,512]{1,0:T(8,128)(2,1)S(1)} collective-permute-done((bf16[512,512]{1,0:T(8,128)(2,1)}, bf16[512,512]{1,0:T(8,128)(2,1)S(1)}, u32[]{:S(2)}, u32[]{:S(2)}) %collective-permute-start) | collective-permute-done | bytes 524320 | tf_op jit(solution)/shard_map/ppermute | solution.py:15
  23.2 1.9 %collective-permute-start.2 = (bf16[512,512]{1,0:T(8,128)(2,1)S(1)}, bf16[512,512]{1,0:T(8,128)(2,1)S(1)}, u32[]{:S(2)}, u32[]{:S(2)}) collective-permute-start(bf16[512,512]{1,0:T(8,128)(2,1)S(1)} %collective-permute-done), channel_id=1, source_target_pairs={{0,8},{8,16},{16,24},{24,32},{32,40},{40,48},{48,56},{56,64},{64,7... | collective-permute-start | bytes 1572872 | tf_op jit(solution)/shard_map/ppermute | solution.py:15
  25.1 0.1 convert_reduce_fusion
  25.2 0.0 collective-permute-done.3
  25.2 1.9 %collective-permute-start.5 = (bf16[512]{0:T(512)(128)(2,1)S(1)}, bf16[512]{0:T(512)(128)(2,1)S(1)}, u32[]{:S(2)}, u32[]{:S(2)}) collective-permute-start(bf16[512]{0:T(512)(128)(2,1)S(1)} %collective-permute-done.3), channel_id=1, source_target_pairs={{0,8},{8,16},{16,24},{24,32},{32,40},{40,48},{48,56},{56,64},{64,7... | collective-permute-start | bytes 3080 | tf_op jit(solution)/shard_map/ppermute | solution.py:15
  27.2 10.5 %collective-permute-done.5 = bf16[512]{0:T(512)(128)(2,1)S(1)} collective-permute-done((bf16[512]{0:T(512)(128)(2,1)S(1)}, bf16[512]{0:T(512)(128)(2,1)S(1)}, u32[]{:S(2)}, u32[]{:S(2)}) %collective-permute-start.5) | collective-permute-done | bytes 1056 | tf_op jit(solution)/shard_map/ppermute | solution.py:15
  37.6 1.5 %convolution_multiply_fusion.2 = f32[512,512]{1,0:T(8,128)S(1)} fusion(bf16[512,512]{1,0:T(8,128)(2,1)} %param.4, bf16[512,512]{1,0:T(8,128)(2,1)S(1)} %collective-permute-done), kind=kOutput, calls=%fused_computation.35 | convolution fusion | flops 268697600 | bytes 2097152 | tf_op jit(solution)/shard_map/dot_general | solution.py:62
  39.2 0.0 collective-permute-done.2
  39.2 0.5 convolution_multiply_fusion.1
  39.7 1.9 %collective-permute-start.4 = (bf16[512,512]{1,0:T(8,128)(2,1)S(1)}, bf16[512,512]{1,0:T(8,128)(2,1)S(1)}, u32[]{:S(2)}, u32[]{:S(2)}) collective-permute-start(bf16[512,512]{1,0:T(8,128)(2,1)S(1)} %collective-permute-done.2), channel_id=1, source_target_pairs={{0,8},{8,16},{16,24},{24,32},{32,40},{40,48},{48,56},{56,64},{64,7... | collective-permute-start | bytes 1572872 | tf_op jit(solution)/shard_map/ppermute | solution.py:15
  41.6 1.6 %fusion.19 = (f32[512,512]{1,0:T(8,128)S(1)}, f32[512,512]{1,0:T(8,128)S(1)}) fusion(f32[512,512]{1,0:T(8,128)S(1)} %convolution_multiply_fusion.1, f32[512]{0:T(512)S(1)} %convert_element_type.42, f32[512]{0:T(512)S(1)} %convert_multiply_fusion, f32[512,512]{1,0:T(8,128)S(1)} %convolution_multiply_fusion.2, f32[512]{0:T(512)S(1)} %convert_element_type.41), kind=kLoop, calls=%fused_computation.50 | loop fusion | flops 2097152 | bytes 4200448 | tf_op jit(solution)/shard_map/add | solution.py:22
  43.2 1.6 %fusion.20 = (f32[512,512]{1,0:T(8,128)S(1)}, f32[512,512]{1,0:T(8,128)S(1)}) fusion(f32[512,512]{1,0:T(8,128)S(1)} %get-tuple-element.21, f32[512]{0:T(512)S(1)} %convert_element_type.42, f32[512]{0:T(512)S(1)} %convert_multiply_fusion, f32[512,512]{1,0:T(8,128)S(1)} %get-tuple-element.22, f32[512]{0:T(512)S(1)} %convert_element_type.41), kind=kLoop, calls=%fused_computation.51 | loop fusion | flops 2097152 | bytes 4200448 | tf_op jit(solution)/shard_map/add | solution.py:22
  44.8 9.2 %collective-permute-done.4 = bf16[512,512]{1,0:T(8,128)(2,1)S(1)} collective-permute-done((bf16[512,512]{1,0:T(8,128)(2,1)S(1)}, bf16[512,512]{1,0:T(8,128)(2,1)S(1)}, u32[]{:S(2)}, u32[]{:S(2)}) %collective-permute-start.4) | collective-permute-done | bytes 524320 | tf_op jit(solution)/shard_map/ppermute | solution.py:15
  54.1 0.5 convolution_multiply_fusion
  54.5 3.6 %fusion.56 = (f32[512]{0:T(512)S(1)}, f32[512,512]{1,0:T(8,128)}, f32[512,512]{1,0:T(8,128)S(1)}, f32[512]{0:T(512)S(1)}, f32[512,512]{1,0:T(8,128)}) fusion(f32[512,512]{1,0:T(8,128)S(1)} %get-tuple-element.19, f32[512]{0:T(512)S(1)} %convert_element_type.42, f32[512]{0:T(512)S(1)} %convert_multiply_fusion, f32[512,512]{1,0:T(8,128)S(1)} %convolution_multiply_fusion, ...), kind=kLoop, calls=%fused_computation.101 | loop fusion | flops 3668992 | bytes 6303744 | tf_op jit(solution)/shard_map/reduce_max | solution.py:71
  58.2 0.8 fusion.23
  59.0 1.0 %fusion.60 = (f32[512]{0:T(512)S(1)}, f32[512,512]{1,0:T(8,128)S(1)}) fusion(f32[512,512]{1,0:T(8,128)S(1)} %fusion.23, f32[512]{0:T(512)S(1)} %convert_element_type.43, f32[512]{0:T(512)S(1)} %convert_multiply_fusion), kind=kLoop, calls=%fused_computation.103 | loop fusion | flops 1310208 | bytes 2103296 | tf_op jit(solution)/shard_map/reduce_max | solution.py:71
  60.0 0.3 copy.13
  60.3 0.0 copy-start.2
  60.3 0.6 copy.14
  60.9 0.6 copy-done.2
  61.5 0.3 copy.11
  61.9 0.6 copy.12
  62.5 1.3 %fusion.48 = f32[8,128,4,128]{3,0,2,1:T(8,128)S(1)} fusion(f32[128,4,128,4]{2,3,1,0:T(4,128)S(1)} %copy.14, s32[8]{0:T(128)S(1)} %get-tuple-element.12, pred[8]{0:T(512)(128)(4,1)S(1)} %get-tuple-element.15), kind=kOutput, calls=%fused_computation.87 | convolution fusion | flops 25165888 | bytes 3145768 | tf_op jit(solution)/shard_map/nr,rpx->npx/dot_general | solution.py:30
  63.8 2.5 %fusion = f32[8,1,128,128]{3,1,2,0:T(1,128)S(1)} fusion(f32[8,128,4,128]{3,0,2,1:T(8,128)S(1)} %fusion.48, pred[8,4,1,1]{1,0,2,3:T(8,128)(4,1)S(1)} %fusion.37), kind=kOutput, calls=%fused_computation | convolution fusion | flops 6291456 | bytes 2621472 | tf_op jit(solution)/shard_map/nc,npcq->npq/dot_general | solution.py:36
  66.3 1.3 %fusion.45 = f32[8,128,4,128]{3,0,2,1:T(8,128)S(1)} fusion(f32[128,4,128,4]{2,3,1,0:T(4,128)S(1)} %copy.12, s32[8]{0:T(128)S(1)} %get-tuple-element.12, pred[8]{0:T(512)(128)(4,1)S(1)} %get-tuple-element.14), kind=kOutput, calls=%fused_computation.85 | convolution fusion | flops 25165888 | bytes 3145768 | tf_op jit(solution)/shard_map/nr,rpx->npx/dot_general | solution.py:30
  67.6 2.3 %fusion.2 = f32[8,1,128,128]{3,1,2,0:T(1,128)S(1)} fusion(f32[8,128,4,128]{3,0,2,1:T(8,128)S(1)} %fusion.45, pred[8,4,1,1]{1,0,2,3:T(8,128)(4,1)S(1)} %fusion.37), kind=kOutput, calls=%fused_computation.2 | convolution fusion | flops 6291456 | bytes 2621472 | tf_op jit(solution)/shard_map/nc,npcq->npq/dot_general | solution.py:36
  69.9 0.0 copy-done.1
  69.9 0.3 copy.9
  70.3 0.6 copy.10
  70.9 1.3 %fusion.42 = f32[8,128,4,128]{3,0,2,1:T(8,128)S(1)} fusion(f32[128,4,128,4]{2,3,1,0:T(4,128)S(1)} %copy.10, s32[8]{0:T(128)S(1)} %get-tuple-element.12, pred[8]{0:T(512)(128)(4,1)S(1)} %get-tuple-element.13), kind=kOutput, calls=%fused_computation.83 | convolution fusion | flops 25165888 | bytes 3145768 | tf_op jit(solution)/shard_map/nr,rpx->npx/dot_general | solution.py:30
  72.2 2.3 %fusion.4 = f32[8,1,128,128]{3,1,2,0:T(1,128)S(1)} fusion(f32[8,128,4,128]{3,0,2,1:T(8,128)S(1)} %fusion.42, pred[8,4,1,1]{1,0,2,3:T(8,128)(4,1)S(1)} %fusion.37), kind=kOutput, calls=%fused_computation.4 | convolution fusion | flops 6291456 | bytes 2621472 | tf_op jit(solution)/shard_map/nc,npcq->npq/dot_general | solution.py:36
  74.5 0.9 fusion.6
  75.4 0.9 copy.15
  76.3 7.4 %all-to-all-start = ((bf16[8,2,128,128]{3,2,1,0:T(8,128)(2,1)}), bf16[8,2,128,128]{3,2,1,0:T(8,128)(2,1)S(1)}, u32[]{:S(2)}, u32[]{:S(2)}) async-start(bf16[8,2,128,128]{3,2,1,0:T(8,128)(2,1)} %copy.15), calls=%async_computation | async-start | bytes 1048576 | tf_op jit(solution)/shard_map/all_to_all | solution.py:95
  83.7 0.6 maximum_maximum_fusion
  84.3 10.1 %all-to-all-done = bf16[8,2,128,128]{3,2,1,0:T(8,128)(2,1)S(1)} async-done(((bf16[8,2,128,128]{3,2,1,0:T(8,128)(2,1)}), bf16[8,2,128,128]{3,2,1,0:T(8,128)(2,1)S(1)}, u32[]{:S(2)}, u32[]{:S(2)}) %all-to-all-start) | async-done | bytes 524320 | tf_op jit(solution)/shard_map/all_to_all | solution.py:95
  94.5 0.8 copy.52
  (7 shorter events, 0.0 us)
Async XLA Ops:
  0.6 38.5 %copy-start = (bf16[512,512]{1,0:T(8,128)(2,1)S(1)}, bf16[512,512]{1,0:T(8,128)(2,1)}, u32[]{:S(2)}) copy-start(bf16[512,512]{1,0:T(8,128)(2,1)} %param.4) | copy-start | bytes 1572868
  0.6 15.0 %collective-permute-start.1 = (bf16[512]{0:T(512)(128)(2,1)}, bf16[512]{0:T(512)(128)(2,1)S(1)}, u32[]{:S(2)}, u32[]{:S(2)}) collective-permute-start(bf16[512]{0:T(512)(128)(2,1)} %param.5), channel_id=1, source_target_pairs={{0,8},{8,16},{16,24},{24,32},{32,40},{40,48},{48,56},{56,64},{64,7... | collective-permute-start | bytes 3080 | tf_op jit(solution)/shard_map/ppermute | solution.py:15
  2.7 20.5 %collective-permute-start = (bf16[512,512]{1,0:T(8,128)(2,1)}, bf16[512,512]{1,0:T(8,128)(2,1)S(1)}, u32[]{:S(2)}, u32[]{:S(2)}) collective-permute-start(bf16[512,512]{1,0:T(8,128)(2,1)} %param.4), channel_id=1, source_target_pairs={{0,8},{8,16},{16,24},{24,32},{32,40},{40,48},{48,56},{56,64},{64,7... | collective-permute-start | bytes 1572872 | tf_op jit(solution)/shard_map/ppermute | solution.py:15
  15.7 9.5 %collective-permute-start.3 = (bf16[512]{0:T(512)(128)(2,1)S(1)}, bf16[512]{0:T(512)(128)(2,1)S(1)}, u32[]{:S(2)}, u32[]{:S(2)}) collective-permute-start(bf16[512]{0:T(512)(128)(2,1)S(1)} %collective-permute-done.1), channel_id=1, source_target_pairs={{0,8},{8,16},{16,24},{24,32},{32,40},{40,48},{48,56},{56,64},{64,7... | collective-permute-start | bytes 3080 | tf_op jit(solution)/shard_map/ppermute | solution.py:15
  23.2 16.0 %collective-permute-start.2 = (bf16[512,512]{1,0:T(8,128)(2,1)S(1)}, bf16[512,512]{1,0:T(8,128)(2,1)S(1)}, u32[]{:S(2)}, u32[]{:S(2)}) collective-permute-start(bf16[512,512]{1,0:T(8,128)(2,1)S(1)} %collective-permute-done), channel_id=1, source_target_pairs={{0,8},{8,16},{16,24},{24,32},{32,40},{40,48},{48,56},{56,64},{64,7... | collective-permute-start | bytes 1572872 | tf_op jit(solution)/shard_map/ppermute | solution.py:15
  25.2 12.4 %collective-permute-start.5 = (bf16[512]{0:T(512)(128)(2,1)S(1)}, bf16[512]{0:T(512)(128)(2,1)S(1)}, u32[]{:S(2)}, u32[]{:S(2)}) collective-permute-start(bf16[512]{0:T(512)(128)(2,1)S(1)} %collective-permute-done.3), channel_id=1, source_target_pairs={{0,8},{8,16},{16,24},{24,32},{32,40},{40,48},{48,56},{56,64},{64,7... | collective-permute-start | bytes 3080 | tf_op jit(solution)/shard_map/ppermute | solution.py:15
  39.7 14.4 %collective-permute-start.4 = (bf16[512,512]{1,0:T(8,128)(2,1)S(1)}, bf16[512,512]{1,0:T(8,128)(2,1)S(1)}, u32[]{:S(2)}, u32[]{:S(2)}) collective-permute-start(bf16[512,512]{1,0:T(8,128)(2,1)S(1)} %collective-permute-done.2), channel_id=1, source_target_pairs={{0,8},{8,16},{16,24},{24,32},{32,40},{40,48},{48,56},{56,64},{64,7... | collective-permute-start | bytes 1572872 | tf_op jit(solution)/shard_map/ppermute | solution.py:15
  60.3 1.2 %copy-start.2 = (f32[512,512]{1,0:T(8,128)S(1)}, f32[512,512]{1,0:T(8,128)}, u32[]{:S(2)}) copy-start(f32[512,512]{1,0:T(8,128)} %get-tuple-element.5) | copy-start | bytes 3145732
  67.6 2.3 %copy-start.1 = (f32[512,512]{1,0:T(8,128)S(1)}, f32[512,512]{1,0:T(8,128)}, u32[]{:S(2)}) copy-start(f32[512,512]{1,0:T(8,128)} %get-tuple-element.18) | copy-start | bytes 3145732
  76.3 18.1 %all-to-all-start = ((bf16[8,2,128,128]{3,2,1,0:T(8,128)(2,1)}), bf16[8,2,128,128]{3,2,1,0:T(8,128)(2,1)S(1)}, u32[]{:S(2)}, u32[]{:S(2)}) async-start(bf16[8,2,128,128]{3,2,1,0:T(8,128)(2,1)} %copy.15), calls=%async_computation | async-start | bytes 1048576 | tf_op jit(solution)/shard_map/all_to_all | solution.py:95
where the time goes:
time: 95.9 us; the launch traced here: 95.3 us
  waiting for transfers between devices  40.9 us (43%)
  starting transfers between devices  21.5 us (22%)
  matrix products  14.3 us (15%)
  other arithmetic  11.7 us (12%)
  local copies, waits for them, and re-layouts  5.93 us (6%)
    ppermute x6, waiting for transfers between devices, from_behind(): return lax.ppermute(value, axis, pairs)  30.8 us
    ppermute x6, starting transfers between devices, from_behind(): return lax.ppermute(value, axis, pairs)  14.1 us
    all_to_all x1, waiting for transfers between devices, body(): lax.all_to_all(bucket, 'grp', split_axis=0, concat_axis=0, tiled=True)  10.1 us
    all_to_all x1, starting transfers between devices, body(): lax.all_to_all(bucket, 'grp', split_axis=0, concat_axis=0, tiled=True)  7.39 us
    dot_general x3, matrix products, select_pieces(): jnp.einsum('nc,npcq->npq', col_hot, picked_rows.reshape(count, PIECE, blo...  7.01 us
    reduce_max x2, other arithmetic, body(): best_score = jnp.maximum(best_score, jnp.max(tile_scores, axis=1))  4.62 us
    add x3, other arithmetic, smooth_tile(): tile_scores + weight_pair * (padded[:-2, :-2] + padded[2:, 2:])  4.06 us
    dot_general x3, matrix products, select_pieces(): jnp.einsum('nr,rpx->npx', row_hot, tile_scores.reshape(blocks, PIECE, fra...  3.95 us
  transfers between devices with their start and end apart: 7, of which 5 were waited for; matrix products, arithmetic and copies ran while one was open for 9% of the time, Pallas kernels for 0%

commit v1 on v0

v1 whole, which is shorter than its diff:
```python
import functools

import jax
import jax.numpy as jnp
from jax import lax
from jax.experimental import pallas as pl
from jax.experimental.pallas import tpu as pltpu
from jax.sharding import PartitionSpec as P

MESH = pl.DeviceIdType.MESH
F = 512
D = 512
PIECE = 128
CAP = 2
ROT = 3
GROUPS = 8
STEP = 65
TALL = 8 * STEP
PAD = 8
CHUNKS = 4
SCALE = D ** (-0.5)


def rotate_left(x, n):
    n %= F
    return x if n == 0 else pltpu.roll(x, F - n, 1)


def four(x):
    return jnp.concatenate([x] * 4, axis=1)


def column_weights(w_ref, slot, acs_ref):
    lane = lax.broadcasted_iota(jnp.int32, (8, 128), 1)
    sub = lax.broadcasted_iota(jnp.int32, (8, F), 0)
    rows = [jnp.broadcast_to(w_ref[slot, c : c + 1, :], (8, 128)) for c in range(4)]
    for k in range(2):
        kept = list(rows)
        if k == 0:
            kept[0] = jnp.where(lane == 0, 0.0, kept[0])
        else:
            kept[3] = jnp.where(lane == 127, 0.0, kept[3])
        x = jnp.concatenate(kept, axis=1)
        for bit in (1, 2, 4):
            x = jnp.where((sub & bit) != 0, rotate_left(x, bit), x)
        for m in range((STEP + 6 + 7) // 8):
            acs_ref[k, 8 * m : 8 * m + 8, :] = rotate_left(x, 8 * m - 3)


def row_weights(w_ref, a_ref):
    for r in range(4):
        wide = jnp.broadcast_to(w_ref[0, r : r + 1, :], (128, 128))
        a_ref[PAD + 128 * r : PAD + 128 * (r + 1), :] = jnp.transpose(wide) * 0.25


def product(r_ref, c_ref, t, s_ref):
    for h in range(2):
        part = lax.dot_general(
            r_ref[...],
            c_ref[t, 256 * h : 256 * (h + 1), :],
            (((1,), (1,)), ((), ())),
            preferred_element_type=jnp.float32,
        )
        for k in range(2):
            s_ref[2 * h + k, PAD : PAD + F, :] = part[:, 128 * k : 128 * (k + 1)]


def smooth(s_ref, a_ref, acs_ref, t_ref, m_ref, t):
    levels, weights = {}, {}

    def level(n, q):
        if (n, q) not in levels:
            if n == 0:
                rows = [s_ref[c, pl.ds(PAD + q, 8, stride=STEP), :] for c in range(4)]
                levels[n, q] = rotate_left(jnp.concatenate(rows, axis=1), q)
            else:
                if q not in weights:
                    a = four(a_ref[pl.ds(PAD + q, 8, stride=STEP), :])
                    weights[q] = (a * acs_ref[0, q + 3 : q + 4, :], a * acs_ref[1, q + 3 : q + 4, :])
                before, after = weights[q]
                levels[n, q] = (
                    level(n - 1, q) + before * level(n - 1, q - 1) + after * level(n - 1, q + 1)
                )
        return levels[n, q]

    for q in range(STEP):
        x = level(3, q)
        widest = jnp.maximum(
            jnp.maximum(x[:, :128], x[:, 128:256]), jnp.maximum(x[:, 256:384], x[:, 384:])
        )
        m_ref[pl.ds(q, 8, stride=STEP), :] = jnp.maximum(m_ref[pl.ds(q, 8, stride=STEP), :], widest)
        x = rotate_left(x, -q)
        for c in range(4):
            t_ref[pl.ds((t * 4 + c) * TALL + q, 8, stride=STEP), :] = x[:, 128 * c : 128 * (c + 1)]


def kernel(
    n_blk,
    emb,
    w_in,
    cand,
    owner,
    out,
    best,
    rows,
    cols,
    wx,
    listing,
    plan,
    s_ref,
    a_ref,
    acs_ref,
    t_ref,
    m_ref,
    bucket,
    top,
    loc,
    e_send,
    e_recv,
    z_send,
    z_recv,
    f_send,
    f_recv,
    y_send,
    w_send,
    w_recv,
    c_sem,
    p_send,
    p_recv,
    b_sem,
):
    b, g = lax.axis_index("blk"), lax.axis_index("grp")
    core = lax.rem(b, 2)
    even, odd = core == 0, core == 1
    home = lax.rem(b + 2 * (1 - core), n_blk)

    def behind(k):
        return (lax.rem(b + k + n_blk, n_blk), g)

    def peer(dx, dy):
        return lax.rem(g // 2 + dx, 4) * 2 + lax.rem(g + dy, 2)

    def remote(src, dst, send, recv, device):
        return pltpu.make_async_remote_copy(
            src_ref=src, dst_ref=dst, send_sem=send, recv_sem=recv, device_id=device, device_id_type=MESH
        )

    barrier = pltpu.get_barrier_semaphore()

    def greet(device):
        pl.semaphore_signal(barrier, inc=1, device_id=device, device_id_type=MESH)

    back = lax.rem(b - 2 * (1 - core) + n_blk, n_blk)
    order = [(0, 1), (2, 1), (1, 1), (3, 1), (2, 0), (1, 0), (3, 0)]

    @pl.when(even)
    def _():
        greet(behind(2))
        greet(behind(1))
        greet(behind(-1))
        greet((back, g))

    @pl.when(odd)
    def _():
        greet(behind(-1))
        greet(behind(-2))
        greet(behind(-3))

    for dx, dy in order:
        greet((back, peer(dx, dy)))

    own_rows = pltpu.make_async_copy(emb, rows, loc.at[0])
    own_cols = pltpu.make_async_copy(emb, cols.at[1], loc.at[0])
    own_list = pltpu.make_async_copy(cand, listing, loc.at[1])

    @pl.when(even)
    def _():
        own_cols.start()

    @pl.when(odd)
    def _():
        own_rows.start()
        own_list.start()

    own_slot = 2 * (1 - core)
    wx[own_slot, 0:4, :] = w_in[...].astype(jnp.float32)

    pl.semaphore_wait(barrier, 11 - core)

    quarter = F // CHUNKS
    to_odd = remote(emb, cols.at[0], e_send.at[0], e_recv.at[1], behind(1))
    to_rows = remote(emb, rows, e_send.at[1], e_recv.at[0], behind(-2))
    to_even = remote(emb, cols.at[0], e_send.at[0], e_recv.at[1], behind(-1))

    def chunk(ref, k):
        return ref.at[pl.ds(k * quarter, quarter)]

    ahead = [
        remote(chunk(emb, k), chunk(cols.at[2], k), z_send.at[k], z_recv.at[k], behind(1))
        for k in range(CHUNKS)
    ]
    passed = [
        remote(chunk(cols.at[2], k), chunk(cols.at[1], k), f_send.at[k], f_recv.at[k], behind(1))
        for k in range(CHUNKS)
    ]
    relay = remote(cols.at[0], cols.at[2], y_send.at[0], e_recv.at[2], behind(2))

    def weight(k, steps, slot):
        return remote(wx.at[own_slot], wx.at[slot], w_send.at[k], w_recv.at[slot], behind(steps))

    w_even = [weight(0, -2, 0), weight(1, 1, 1), weight(2, 3, 3)]
    w_odd = [weight(0, -1, 1), weight(1, 1, 3), weight(2, 2, 2)]
    lists = remote(cand, listing, c_sem.at[0], c_sem.at[1], behind(-2))

    @pl.when(even)
    def _():
        lists.start()
        for copy in w_even:
            copy.start()
        to_rows.start()
        to_odd.start()

    @pl.when(odd)
    def _():
        for copy in w_odd:
            copy.start()
        for copy in ahead:
            copy.start()
        to_even.start()

    s_ref[:, 0:PAD, :] = jnp.zeros((4, PAD, 128), jnp.float32)
    s_ref[:, PAD + F :, :] = jnp.zeros((4, s_ref.shape[1] - PAD - F, 128), jnp.float32)
    a_ref[0:PAD, :] = jnp.zeros((PAD, 128), jnp.float32)
    a_ref[PAD + F :, :] = jnp.zeros((a_ref.shape[0] - PAD - F, 128), jnp.float32)
    m_ref[...] = jnp.full_like(m_ref, -jnp.inf)

    @pl.when(even)
    def _():
        own_cols.wait()
        weight(0, -2, 0).wait_recv()
        lists.wait_recv()

    @pl.when(odd)
    def _():
        own_rows.wait()
        own_list.wait()
        weight(2, 2, 2).wait_recv()

    weight(1, 1, 1).wait_recv()
    weight(1, 1, 3).wait_recv()
    row_weights(wx, a_ref)
    for t in range(ROT):
        column_weights(wx, t + 1, acs_ref.at[t])

    count = listing.shape[1]
    where, slot_of, start_of = [], [], []
    for n in range(count):
        where.append(owner[listing[3, n]])
        start_of.append(
            (jnp.maximum(listing[0, n] - 1, 0) * 4 + listing[2, n]) * STEP + listing[1, n] * (PIECE // 8)
        )
        slot = jnp.int32(0)
        for m in range(n):
            slot = slot + jnp.where(where[m] == where[n], 1, 0)
        slot_of.append(slot)
    for d in range(GROUPS):
        for s in range(CAP):
            start, there = jnp.int32(0), jnp.int32(0)
            for n in range(count):
                here = (where[n] == d) & (slot_of[n] == s)
                start = jnp.where(here, start_of[n], start)
                there = jnp.where(here, 1, there)
            plan[0, d * CAP + s] = start
            plan[1, d * CAP + s] = there

    @pl.when(even)
    def _():
        for k in range(CHUNKS):
            ahead[k].wait_recv()
            passed[k].start()
        to_rows.wait_recv()

    to_even.wait_recv()

    @pl.when(odd)
    def _():
        ahead[CHUNKS - 2].wait_send()
        relay.start()

    def tile(t, carry):
        @pl.when(odd & (t == 1))
        def _():
            for k in range(CHUNKS):
                passed[k].wait_recv()

        @pl.when(odd & (t == 2))
        def _():
            relay.wait_recv()

        product(rows, cols, t, s_ref)
        smooth(s_ref, a_ref, acs_ref.at[t], t_ref, m_ref, t)
        return carry

    lax.fori_loop(0, ROT, tile, 0)

    def fill(d):
        for s in range(CAP):
            piece = t_ref[pl.ds(plan[0, d * CAP + s] * 8, PIECE), :]
            there = jnp.broadcast_to(plan[1, d * CAP + s], (PIECE, PIECE)) > 0
            piece = jnp.where(there, piece * SCALE, 0.0)
            bucket[d, PIECE * s : PIECE * (s + 1), :] = piece.astype(jnp.bfloat16)

    def piece_copy(d):
        return remote(bucket.at[d], out.at[g], p_send.at[d], p_recv.at[g], (home, d))

    for dx, dy in order:
        d = peer(dx, dy)
        fill(d)
        piece_copy(d).start()
    fill(g)
    own_piece = pltpu.make_async_copy(bucket.at[g], out.at[g], loc.at[0])

    @pl.when(even)
    def _():
        piece_copy(g).start()

    @pl.when(odd)
    def _():
        own_piece.start()

    for r in range(4):
        block = jnp.transpose(m_ref[128 * r : 128 * (r + 1), :])
        top[r : r + 1, :] = jnp.max(block, axis=0, keepdims=True) * SCALE
    top_home = remote(top, best, b_sem.at[0], b_sem.at[1], behind(2))
    top_here = pltpu.make_async_copy(top, best, loc.at[1])

    @pl.when(even)
    def _():
        top_home.start()

    @pl.when(odd)
    def _():
        top_here.start()

    @pl.when(even)
    def _():
        for copy in w_even:
            copy.wait_send()
        lists.wait_send()
        to_rows.wait_send()
        to_odd.wait_send()
        for copy in passed:
            copy.wait_send()
        top_home.wait()
        piece_copy(g).wait_send()
        piece_copy(g).wait_recv()

    @pl.when(odd)
    def _():
        for copy in w_odd:
            copy.wait_send()
        for k in range(CHUNKS):
            if k != CHUNKS - 2:
                ahead[k].wait_send()
        to_even.wait_send()
        relay.wait_send()
        top_here.wait()
        own_piece.wait()

    for dx, dy in order:
        d = peer(dx, dy)
        piece_copy(d).wait_send()
        remote(bucket.at[d], out.at[d], p_send.at[d], p_recv.at[d], (home, d)).wait_recv()


def body(n_blk, embeddings, frame_weight, candidates, owner):
    count = candidates.shape[3]
    dma = pltpu.SemaphoreType.DMA
    any_, vmem, smem = (pl.BlockSpec(memory_space=m) for m in (pl.ANY, pltpu.VMEM, pltpu.SMEM))
    out, best = pl.pallas_call(
        functools.partial(kernel, n_blk),
        out_shape=(
            jax.ShapeDtypeStruct((GROUPS, CAP * PIECE, PIECE), jnp.bfloat16),
            jax.ShapeDtypeStruct((4, 128), jnp.float32),
        ),
        in_specs=[any_, vmem, any_, smem],
        out_specs=(any_, any_),
        scratch_shapes=[
            pltpu.VMEM((F, D), jnp.bfloat16),
            pltpu.VMEM((ROT, F, D), jnp.bfloat16),
            pltpu.VMEM((4, 8, 128), jnp.float32),
            pltpu.SMEM((4, count), jnp.int32),
            pltpu.SMEM((2, GROUPS * CAP), jnp.int32),
            pltpu.VMEM((4, TALL + 2 * PAD, 128), jnp.float32),
            pltpu.VMEM((TALL + 2 * PAD, 128), jnp.float32),
            pltpu.VMEM((ROT, 2, (STEP + 6 + 7) // 8 * 8, F), jnp.float32),
            pltpu.VMEM((ROT * 4 * TALL, 128), jnp.float32),
            pltpu.VMEM((TALL, 128), jnp.float32),
            pltpu.VMEM((GROUPS, CAP * PIECE, PIECE), jnp.bfloat16),
            pltpu.VMEM((4, 128), jnp.float32),
            dma((2,)),
            dma((2,)),
            dma((3,)),
            dma((CHUNKS,)),
            dma((CHUNKS,)),
            dma((CHUNKS,)),
            dma((CHUNKS,)),
            dma((1,)),
            dma((3,)),
            dma((4,)),
            dma((2,)),
            dma((GROUPS,)),
            dma((GROUPS,)),
            dma((2,)),
        ],
        compiler_params=pltpu.CompilerParams(
            collective_id=0, has_side_effects=True, vmem_limit_bytes=40 << 20
        ),
        name="window_join",
    )(embeddings, frame_weight.reshape(4, 128), candidates.reshape(4, count), owner)
    return best.reshape(F), out.reshape(1, 1, GROUPS, CAP, PIECE, PIECE)


def solution(mesh):
    return jax.shard_map(
        functools.partial(body, mesh.shape["blk"]),
        mesh=mesh,
        in_specs=(P(("blk", "grp"), None), P(("blk", "grp")), P("blk", "grp", None, None), P()),
        out_specs=(P(("blk", "grp")), P("blk", "grp", None, None, None, None)),
        check_vma=False,
    )
```

time: 95.9 us -> 51.6 us (0.54)
  the two profiles are of different devices: /device:TPU:2 before, /device:TPU:8 now
where the time goes in v1:
time: 51.6 us; the launch traced here: 51.3 us
  Pallas kernels  46.9 us (91%)
  local copies, waits for them, and re-layouts  3.77 us (7%)
  between operations  0.66 us (1%)
    pallas_call x1, Pallas kernels, body(): pl.pallas_call(functools.partial(kernel, n_blk), out_shape=(jax.ShapeDtyp...  46.9 us
    unnamed x10, local copies, waits for them, and re-layouts  3.77 us

profile of v1, /device:TPU:8, one launch (start us, length us, event | category | flops | bytes accessed | tf_op | source)
XLA Modules:
  0.0 51.3 jit_solution(9354663585767094944)
XLA Ops:
  0.6 0.0 copy-start.1
  0.6 0.0 copy-start.3
  0.7 0.7 %copy-done.1 = s32[1,1,4,8]{3,2,1,0:T(4,128)S(1)} copy-done((s32[1,1,4,8]{3,2,1,0:T(4,128)S(1)}, s32[1,1,4,8]{3,2,1,0:T(4,128)}, u32[]{:S(2)}) %copy-start.1) | copy-done | bytes 152
  1.3 0.0 copy-done.3
  1.3 0.0 copy-start
  1.3 1.0 %copy-done = bf16[512,512]{1,0:T(8,128)(2,1)S(1)} copy-done((bf16[512,512]{1,0:T(8,128)(2,1)S(1)}, bf16[512,512]{1,0:T(8,128)(2,1)}, u32[]{:S(2)}) %copy-start) | copy-done | bytes 524312
  2.4 0.0 copy-start.2
  2.4 0.7 %copy-done.2 = s32[512]{0:T(512)S(1)} copy-done((s32[512]{0:T(512)S(1)}, s32[512]{0:T(512)}, u32[]{:S(2)}) %copy-start.2) | copy-done | bytes 2072
  3.1 46.9 %window_join.1 = (bf16[8,256,128]{2,1,0:T(8,128)(2,1)S(1)}, f32[4,128]{1,0:T(4,128)S(1)}) custom-call(bf16[512,512]{1,0:T(8,128)(2,1)S(1)} %copy-done, bf16[4,128]{1,0:T(4,128)(2,1)S(1)} %bitcast.7, s32[4,8]{1,0:T(4,128)S(1)} %bitcast.5, s32[512]{0:T(512)S(1)} %copy-done.2), custom_call_target="tpu_custom_call" | custom-call | tf_op jit(solution)/shard_map/window_join/pallas_call | solution.py:380
  50.0 0.6 %copy.8 = f32[512]{0:T(512)} copy(f32[512]{0:T(512)S(1)} %bitcast.6) | data formatting | bytes 4096
  50.5 0.8 %copy.9 = bf16[1,1,8,2,128,128]{5,4,3,2,1,0:T(8,128)(2,1)} copy(bf16[1,1,8,2,128,128]{5,4,3,2,1,0:T(8,128)(2,1)S(1)} %bitcast.4) | data formatting | bytes 1048576
Async XLA Ops:
  0.6 0.7 %copy-start.1 = (s32[1,1,4,8]{3,2,1,0:T(4,128)S(1)}, s32[1,1,4,8]{3,2,1,0:T(4,128)}, u32[]{:S(2)}) copy-start(s32[1,1,4,8]{3,2,1,0:T(4,128)} %param.6) | copy-start | bytes 388
  0.6 0.7 %copy-start.3 = (bf16[512]{0:T(512)(128)(2,1)S(1)}, bf16[512]{0:T(512)(128)(2,1)}, u32[]{:S(2)}) copy-start(bf16[512]{0:T(512)(128)(2,1)} %param.5) | copy-start | bytes 3076
  1.3 1.0 %copy-start = (bf16[512,512]{1,0:T(8,128)(2,1)S(1)}, bf16[512,512]{1,0:T(8,128)(2,1)}, u32[]{:S(2)}) copy-start(bf16[512,512]{1,0:T(8,128)(2,1)} %emb.1) | copy-start | bytes 1572868
  2.4 0.7 %copy-start.2 = (s32[512]{0:T(512)S(1)}, s32[512]{0:T(512)}, u32[]{:S(2)}) copy-start(s32[512]{0:T(512)} %owner.1) | copy-start | bytes 6148

commit v2 on v1

--- a/solution.py
+++ b/solution.py
@@ -99,9 +99,12 @@
     emb,
     w_in,
     cand,
-    owner,
+    owner_in,
     out,
     best,
+    owner,
+    w_own,
+    flood,
     rows,
     cols,
     wx,
@@ -146,19 +149,21 @@
         )
 
     barrier = pltpu.get_barrier_semaphore()
-
-    def greet(device):
-        pl.semaphore_signal(barrier, inc=1, device_id=device, device_id_type=MESH)
-
-    back = lax.rem(b - 2 * (1 - core) + n_blk, n_blk)
     order = [(0, 1), (2, 1), (1, 1), (3, 1), (2, 0), (1, 0), (3, 0)]
-
-    @pl.when(even)
-    def _():
-        greet(behind(2))
+    per_row = n_blk // 4
+    turn = 1 - 2 * lax.rem(g, 2)
+    y_lo = b // per_row
+    y_down = (lax.rem(b - per_row + n_blk, n_blk), g + jnp.where(y_lo == 0, turn, 0))
+    y_up = (lax.rem(b + per_row, n_blk), g + jnp.where(y_lo == 3, turn, 0))
+
+    def greet(device, semaphore=barrier):
+        pl.semaphore_signal(semaphore, inc=1, device_id=device, device_id_type=MESH)
+
+    @pl.when(even)
+    def _():
+        greet(behind(-2))
         greet(behind(1))
         greet(behind(-1))
-        greet((back, g))
 
     @pl.when(odd)
     def _():
@@ -166,12 +171,16 @@
         greet(behind(-2))
         greet(behind(-3))
 
-    for dx, dy in order:
-        greet((back, peer(dx, dy)))
+    greet((b, peer(1, 0)))
+    greet((b, peer(3, 0)))
+    greet(y_up)
 
     own_rows = pltpu.make_async_copy(emb, rows, loc.at[0])
     own_cols = pltpu.make_async_copy(emb, cols.at[1], loc.at[0])
     own_list = pltpu.make_async_copy(cand, listing, loc.at[1])
+    own_weights = pltpu.make_async_copy(w_in, w_own, loc.at[2])
+    owners = pltpu.make_async_copy(owner_in, owner, loc.at[3])
+    own_weights.start()
 
     @pl.when(even)
     def _():
@@ -182,10 +191,9 @@
         own_rows.start()
         own_list.start()
 
+    owners.start()
     own_slot = 2 * (1 - core)
-    wx[own_slot, 0:4, :] = w_in[...].astype(jnp.float32)
-
-    pl.semaphore_wait(barrier, 11 - core)
+    pl.semaphore_wait(barrier, 6)
 
     quarter = F // CHUNKS
     to_odd = remote(emb, cols.at[0], e_send.at[0], e_recv.at[1], behind(1))
@@ -212,21 +220,66 @@
     w_odd = [weight(0, -1, 1), weight(1, 1, 3), weight(2, 2, 2)]
     lists = remote(cand, listing, c_sem.at[0], c_sem.at[1], behind(-2))
 
-    @pl.when(even)
-    def _():
+    first = lax.rem(b // 2, 8) == 0
+    last = lax.rem(b // 2, 8) == 7
+
+    def send_rows():
+        hear(6)
+        to_rows.start()
         lists.start()
-        for copy in w_even:
-            copy.start()
-        to_rows.start()
+        w_even[0].start()
+
+    def hear(k):
+        pl.semaphore_wait(flood.at[k], 1)
+
+    @pl.when(even)
+    def _():
+        greet(behind(2), flood.at[6])
         to_odd.start()
 
     @pl.when(odd)
     def _():
-        for copy in w_odd:
-            copy.start()
         for copy in ahead:
             copy.start()
         to_even.start()
+
+    greet((b, peer(3, 0)), flood.at[0])
+    own_weights.wait()
+    wx[own_slot, 0:4, :] = w_own[...].astype(jnp.float32)
+
+    @pl.when(even)
+    def _():
+        for copy in w_even[1:]:
+            copy.start()
+
+    @pl.when(odd)
+    def _():
+        for copy in w_odd:
+            copy.start()
+
+    pl.when(even & jnp.logical_not(first))(send_rows)
+    for k in range(4):
+        hear(k)
+        greet(y_down, flood.at[k + 1])
+    hear(4)
+
+    @pl.when(even & jnp.logical_not(first))
+    def _():
+        greet(behind(-2), flood.at[5])
+        hear(5)
+
+    @pl.when(even & first)
+    def _():
+        hear(5)
+        send_rows()
+        greet(behind(-2), flood.at[5])
+
+    to_even.wait_recv()
+
+    @pl.when(odd)
+    def _():
+        ahead[CHUNKS - 2].wait_send()
+        relay.start()
 
     s_ref[:, 0:PAD, :] = jnp.zeros((4, PAD, 128), jnp.float32)
     s_ref[:, PAD + F :, :] = jnp.zeros((4, s_ref.shape[1] - PAD - F, 128), jnp.float32)
@@ -248,6 +301,7 @@
 
     weight(1, 1, 1).wait_recv()
     weight(1, 1, 3).wait_recv()
+    owners.wait()
     row_weights(wx, a_ref)
     for t in range(ROT):
         column_weights(wx, t + 1, acs_ref.at[t])
@@ -273,21 +327,15 @@
             plan[0, d * CAP + s] = start
             plan[1, d * CAP + s] = there
 
-    @pl.when(even)
-    def _():
-        for k in range(CHUNKS):
-            ahead[k].wait_recv()
-            passed[k].start()
-        to_rows.wait_recv()
-
-    to_even.wait_recv()
-
-    @pl.when(odd)
-    def _():
-        ahead[CHUNKS - 2].wait_send()
-        relay.start()
+    pl.when(even)(to_rows.wait_recv)
 
     def tile(t, carry):
+        @pl.when(even & (t == 1 + first.astype(jnp.int32)))
+        def _():
+            for k in range(CHUNKS):
+                ahead[k].wait_recv()
+                passed[k].start()
+
         @pl.when(odd & (t == 1))
         def _():
             for k in range(CHUNKS):
@@ -313,6 +361,7 @@
     def piece_copy(d):
         return remote(bucket.at[d], out.at[g], p_send.at[d], p_recv.at[g], (home, d))
 
+    pl.when(odd & last)(functools.partial(hear, 7))
     for dx, dy in order:
         d = peer(dx, dy)
         fill(d)
@@ -341,6 +390,13 @@
     @pl.when(odd)
     def _():
         top_here.start()
+
+    for dx, dy in order:
+        piece_copy(peer(dx, dy)).wait_send()
+
+    @pl.when(even & last)
+    def _():
+        greet(behind(1), flood.at[7])
 
     @pl.when(even)
     def _():
@@ -369,23 +425,25 @@
 
     for dx, dy in order:
         d = peer(dx, dy)
-        piece_copy(d).wait_send()
         remote(bucket.at[d], out.at[d], p_send.at[d], p_recv.at[d], (home, d)).wait_recv()
 
 
 def body(n_blk, embeddings, frame_weight, candidates, owner):
     count = candidates.shape[3]
     dma = pltpu.SemaphoreType.DMA
-    any_, vmem, smem = (pl.BlockSpec(memory_space=m) for m in (pl.ANY, pltpu.VMEM, pltpu.SMEM))
+    hbm, vmem = (pl.BlockSpec(memory_space=m) for m in (pltpu.HBM, pltpu.VMEM))
     out, best = pl.pallas_call(
         functools.partial(kernel, n_blk),
         out_shape=(
             jax.ShapeDtypeStruct((GROUPS, CAP * PIECE, PIECE), jnp.bfloat16),
             jax.ShapeDtypeStruct((4, 128), jnp.float32),
         ),
-        in_specs=[any_, vmem, any_, smem],
-        out_specs=(any_, any_),
+        in_specs=[hbm] * 4,
+        out_specs=(vmem, vmem),
         scratch_shapes=[
+            pltpu.SMEM(owner.shape, jnp.int32),
+            pltpu.VMEM((4, 128), jnp.bfloat16),
+            pltpu.SemaphoreType.REGULAR((8,)),
             pltpu.VMEM((F, D), jnp.bfloat16),
             pltpu.VMEM((ROT, F, D), jnp.bfloat16),
             pltpu.VMEM((4, 8, 128), jnp.float32),
@@ -398,7 +456,7 @@
             pltpu.VMEM((TALL, 128), jnp.float32),
             pltpu.VMEM((GROUPS, CAP * PIECE, PIECE), jnp.bfloat16),
             pltpu.VMEM((4, 128), jnp.float32),
-            dma((2,)),
+            dma((4,)),
             dma((2,)),
             dma((3,)),
             dma((CHUNKS,)),
@@ -417,7 +475,10 @@
             collective_id=0, has_side_effects=True, vmem_limit_bytes=40 << 20
         ),
         name="window_join",
-    )(embeddings, frame_weight.reshape(4, 128), candidates.reshape(4, count), owner)
+    )(*(
+        pltpu.with_memory_space_constraint(x, pltpu.HBM)
+        for x in (embeddings, frame_weight.reshape(4, 128), candidates.reshape(4, count), owner)
+    ))
     return best.reshape(F), out.reshape(1, 1, GROUPS, CAP, PIECE, PIECE)
 
 

time: 51.6 us -> 46.9 us (0.909)
  the two profiles are of different devices: /device:TPU:8 before, /device:TPU:2 now
where the time goes in v2:
time: 46.9 us; the launch traced here: 46.8 us
  Pallas kernels  44.8 us (96%)
  local copies, waits for them, and re-layouts  1.37 us (3%)
  between operations  0.64 us (1%)
    pallas_call x1, Pallas kernels, body(): pl.pallas_call(functools.partial(kernel, n_blk), out_shape=(jax.ShapeDtyp...  44.8 us
    unnamed x2, local copies, waits for them, and re-layouts  1.37 us

profile of v2, /device:TPU:2, one launch (start us, length us, event | category | flops | bytes accessed | tf_op | source)
XLA Modules:
  0.0 46.8 jit_solution(12034366973998876223)
XLA Ops:
  0.6 44.8 %window_join.1 = (bf16[8,256,128]{2,1,0:T(8,128)(2,1)S(1)}, f32[4,128]{1,0:T(4,128)S(1)}) custom-call(bf16[512,512]{1,0:T(8,128)(2,1)} %emb.1, bf16[4,128]{1,0:T(4,128)(2,1)} %bitcast.7, s32[4,8]{1,0:T(4,128)} %bitcast.6, s32[512]{0:T(512)} %owner_in.1), custom_call_target="tpu_custom_call" | custom-call | tf_op jit(solution)/shard_map/window_join/pallas_call | solution.py:435
  45.4 0.6 %copy.8 = f32[512]{0:T(512)} copy(f32[512]{0:T(512)S(1)} %bitcast.5) | data formatting | bytes 4096
  46.0 0.8 %copy.9 = bf16[1,1,8,2,128,128]{5,4,3,2,1,0:T(8,128)(2,1)} copy(bf16[1,1,8,2,128,128]{5,4,3,2,1,0:T(8,128)(2,1)S(1)} %bitcast.4) | data formatting | bytes 1048576

commit v3 on v2

--- a/solution.py
+++ b/solution.py
@@ -15,8 +15,9 @@
 ROT = 3
 GROUPS = 8
 STEP = 65
-TALL = 8 * STEP
-PAD = 8
+HALF_STEP = 33
+PAD = 16
+TALL = PAD + 8 * STEP
 CHUNKS = 4
 SCALE = D ** (-0.5)
 
@@ -53,45 +54,50 @@
         a_ref[PAD + 128 * r : PAD + 128 * (r + 1), :] = jnp.transpose(wide) * 0.25
 
 
-def product(r_ref, c_ref, t, s_ref):
+def product(r_ref, c_ref, t, s_ref, row, count):
     for h in range(2):
         part = lax.dot_general(
-            r_ref[...],
+            r_ref[pl.ds(row, count), :],
             c_ref[t, 256 * h : 256 * (h + 1), :],
             (((1,), (1,)), ((), ())),
             preferred_element_type=jnp.float32,
         )
         for k in range(2):
-            s_ref[2 * h + k, PAD : PAD + F, :] = part[:, 128 * k : 128 * (k + 1)]
-
-
-def smooth(s_ref, a_ref, acs_ref, t_ref, m_ref, t):
+            s_ref[t, 2 * h + k, pl.ds(PAD + row, count), :] = part[:, 128 * k : 128 * (k + 1)]
+
+
+def smooth(s_ref, a_ref, acs_ref, t_ref, m_ref, t, row, step):
     levels, weights = {}, {}
 
     def level(n, q):
         if (n, q) not in levels:
             if n == 0:
-                rows = [s_ref[c, pl.ds(PAD + q, 8, stride=STEP), :] for c in range(4)]
+                rows = [s_ref[t, c, pl.ds(PAD + row + q, 8, stride=step), :] for c in range(4)]
                 levels[n, q] = rotate_left(jnp.concatenate(rows, axis=1), q)
             else:
                 if q not in weights:
-                    a = four(a_ref[pl.ds(PAD + q, 8, stride=STEP), :])
-                    weights[q] = (a * acs_ref[0, q + 3 : q + 4, :], a * acs_ref[1, q + 3 : q + 4, :])
+                    a = four(a_ref[pl.ds(PAD + row + q, 8, stride=step), :])
+                    weights[q] = (
+                        a * acs_ref[t, 0, q + 3 : q + 4, :],
+                        a * acs_ref[t, 1, q + 3 : q + 4, :],
+                    )
                 before, after = weights[q]
                 levels[n, q] = (
                     level(n - 1, q) + before * level(n - 1, q - 1) + after * level(n - 1, q + 1)
                 )
         return levels[n, q]
 
-    for q in range(STEP):
+    for q in range(step):
         x = level(3, q)
         widest = jnp.maximum(
             jnp.maximum(x[:, :128], x[:, 128:256]), jnp.maximum(x[:, 256:384], x[:, 384:])
         )
-        m_ref[pl.ds(q, 8, stride=STEP), :] = jnp.maximum(m_ref[pl.ds(q, 8, stride=STEP), :], widest)
+        where = pl.ds(PAD + row + q, 8, stride=step)
+        m_ref[where, :] = jnp.maximum(m_ref[where, :], widest)
         x = rotate_left(x, -q)
         for c in range(4):
-            t_ref[pl.ds((t * 4 + c) * TALL + q, 8, stride=STEP), :] = x[:, 128 * c : 128 * (c + 1)]
+            where = pl.ds((t * 4 + c) * TALL + PAD + row + q, 8, stride=step)
+            t_ref[where, :] = x[:, 128 * c : 128 * (c + 1)]
 
 
 def kernel(
@@ -120,6 +126,8 @@
     loc,
     e_send,
     e_recv,
+    r_send,
+    r_recv,
     z_send,
     z_recv,
     f_send,
@@ -193,11 +201,19 @@
 
     owners.start()
     own_slot = 2 * (1 - core)
+    own_weights.wait()
+    wx[own_slot, 0:4, :] = w_own[...].astype(jnp.float32)
     pl.semaphore_wait(barrier, 6)
 
     quarter = F // CHUNKS
     to_odd = remote(emb, cols.at[0], e_send.at[0], e_recv.at[1], behind(1))
-    to_rows = remote(emb, rows, e_send.at[1], e_recv.at[0], behind(-2))
+    half = F // 2
+    to_rows = [
+        remote(
+            emb.at[pl.ds(k * half, half)], rows.at[pl.ds(k * half, half)], r_send.at[k], r_recv.at[k], behind(-2)
+        )
+        for k in range(2)
+    ]
     to_even = remote(emb, cols.at[0], e_send.at[0], e_recv.at[1], behind(-1))
 
     def chunk(ref, k):
@@ -225,9 +241,10 @@
 
     def send_rows():
         hear(6)
-        to_rows.start()
+        w_even[0].start()
         lists.start()
-        w_even[0].start()
+        for copy in to_rows:
+            copy.start()
 
     def hear(k):
         pl.semaphore_wait(flood.at[k], 1)
@@ -235,44 +252,32 @@
     @pl.when(even)
     def _():
         greet(behind(2), flood.at[6])
+        for copy in w_even[1:]:
+            copy.start()
         to_odd.start()
 
     @pl.when(odd)
     def _():
+        for copy in w_odd:
+            copy.start()
+        to_even.start()
         for copy in ahead:
             copy.start()
-        to_even.start()
 
     greet((b, peer(3, 0)), flood.at[0])
-    own_weights.wait()
-    wx[own_slot, 0:4, :] = w_own[...].astype(jnp.float32)
-
-    @pl.when(even)
-    def _():
-        for copy in w_even[1:]:
-            copy.start()
-
-    @pl.when(odd)
-    def _():
-        for copy in w_odd:
-            copy.start()
-
     pl.when(even & jnp.logical_not(first))(send_rows)
     for k in range(4):
         hear(k)
         greet(y_down, flood.at[k + 1])
-    hear(4)
-
-    @pl.when(even & jnp.logical_not(first))
-    def _():
+
+    def tell_behind():
+        hear(4)
         greet(behind(-2), flood.at[5])
-        hear(5)
 
     @pl.when(even & first)
     def _():
-        hear(5)
         send_rows()
-        greet(behind(-2), flood.at[5])
+        tell_behind()
 
     to_even.wait_recv()
 
@@ -281,8 +286,8 @@
         ahead[CHUNKS - 2].wait_send()
         relay.start()
 
-    s_ref[:, 0:PAD, :] = jnp.zeros((4, PAD, 128), jnp.float32)
-    s_ref[:, PAD + F :, :] = jnp.zeros((4, s_ref.shape[1] - PAD - F, 128), jnp.float32)
+    s_ref[:, :, 0:PAD, :] = jnp.zeros((ROT, 4, PAD, 128), jnp.float32)
+    s_ref[:, :, PAD + F :, :] = jnp.zeros((ROT, 4, s_ref.shape[2] - PAD - F, 128), jnp.float32)
     a_ref[0:PAD, :] = jnp.zeros((PAD, 128), jnp.float32)
     a_ref[PAD + F :, :] = jnp.zeros((a_ref.shape[0] - PAD - F, 128), jnp.float32)
     m_ref[...] = jnp.full_like(m_ref, -jnp.inf)
@@ -311,7 +316,7 @@
     for n in range(count):
         where.append(owner[listing[3, n]])
         start_of.append(
-            (jnp.maximum(listing[0, n] - 1, 0) * 4 + listing[2, n]) * STEP + listing[1, n] * (PIECE // 8)
+            (jnp.maximum(listing[0, n] - 1, 0) * 4 + listing[2, n]) * (TALL // 8) + PAD // 8 + listing[1, n] * (PIECE // 8)
         )
         slot = jnp.int32(0)
         for m in range(n):
@@ -327,29 +332,52 @@
             plan[0, d * CAP + s] = start
             plan[1, d * CAP + s] = there
 
-    pl.when(even)(to_rows.wait_recv)
+    def half_tile(k, carry):
+        h = jnp.where(first, jnp.where(k < 4, k // 2, k - 4), k // 3)
+        t = jnp.where(first, jnp.where(k < 4, lax.rem(k, 2), 2), lax.rem(k, 3))
+
+        @pl.when((t == 0) & (h == 0))
+        def _():
+            to_rows[0].wait_recv()
+
+        @pl.when((t == 0) & (h == 1))
+        def _():
+            to_rows[1].wait_recv()
+
+        @pl.when((t == 2) & (h == 0))
+        def _():
+            for c in range(CHUNKS):
+                ahead[c].wait_recv()
+                passed[c].start()
+
+        pl.when((k == 2) & jnp.logical_not(first))(tell_behind)
+        pl.when(k == 4)(functools.partial(hear, 5))
+        product(rows, cols, t, s_ref, h * half, half)
+        smooth(s_ref, a_ref, acs_ref, t_ref, m_ref, t, h * (F - 8 * HALF_STEP + 12) - 12, HALF_STEP)
+        return carry
 
     def tile(t, carry):
-        @pl.when(even & (t == 1 + first.astype(jnp.int32)))
+        @pl.when(t == 1)
         def _():
-            for k in range(CHUNKS):
-                ahead[k].wait_recv()
-                passed[k].start()
-
-        @pl.when(odd & (t == 1))
+            for c in range(CHUNKS):
+                passed[c].wait_recv()
+
+        @pl.when(t == 2)
         def _():
-            for k in range(CHUNKS):
-                passed[k].wait_recv()
-
-        @pl.when(odd & (t == 2))
-        def _():
+            hear(4)
             relay.wait_recv()
 
-        product(rows, cols, t, s_ref)
-        smooth(s_ref, a_ref, acs_ref.at[t], t_ref, m_ref, t)
+        product(rows, cols, t, s_ref, 0, F)
+        smooth(s_ref, a_ref, acs_ref, t_ref, m_ref, t, 0, STEP)
         return carry
 
-    lax.fori_loop(0, ROT, tile, 0)
+    @pl.when(even)
+    def _():
+        lax.fori_loop(0, 2 * ROT, half_tile, 0)
+
+    @pl.when(odd)
+    def _():
+        lax.fori_loop(0, ROT, tile, 0)
 
     def fill(d):
         for s in range(CAP):
@@ -378,7 +406,7 @@
         own_piece.start()
 
     for r in range(4):
-        block = jnp.transpose(m_ref[128 * r : 128 * (r + 1), :])
+        block = jnp.transpose(m_ref[PAD + 128 * r : PAD + 128 * (r + 1), :])
         top[r : r + 1, :] = jnp.max(block, axis=0, keepdims=True) * SCALE
     top_home = remote(top, best, b_sem.at[0], b_sem.at[1], behind(2))
     top_here = pltpu.make_async_copy(top, best, loc.at[1])
@@ -403,7 +431,8 @@
         for copy in w_even:
             copy.wait_send()
         lists.wait_send()
-        to_rows.wait_send()
+        for copy in to_rows:
+            copy.wait_send()
         to_odd.wait_send()
         for copy in passed:
             copy.wait_send()
@@ -426,6 +455,17 @@
     for dx, dy in order:
         d = peer(dx, dy)
         remote(bucket.at[d], out.at[d], p_send.at[d], p_recv.at[d], (home, d)).wait_recv()
+
+
+def settle(out_in, best_in, out, best, sems):
+    copies = [
+        pltpu.make_async_copy(out_in, out, sems.at[0]),
+        pltpu.make_async_copy(best_in, best, sems.at[1]),
+    ]
+    for copy in copies:
+        copy.start()
+    for copy in copies:
+        copy.wait()
 
 
 def body(n_blk, embeddings, frame_weight, candidates, owner):
@@ -449,16 +489,18 @@
             pltpu.VMEM((4, 8, 128), jnp.float32),
             pltpu.SMEM((4, count), jnp.int32),
             pltpu.SMEM((2, GROUPS * CAP), jnp.int32),
-            pltpu.VMEM((4, TALL + 2 * PAD, 128), jnp.float32),
-            pltpu.VMEM((TALL + 2 * PAD, 128), jnp.float32),
+            pltpu.VMEM((ROT, 4, TALL + PAD, 128), jnp.float32),
+            pltpu.VMEM((TALL + PAD, 128), jnp.float32),
             pltpu.VMEM((ROT, 2, (STEP + 6 + 7) // 8 * 8, F), jnp.float32),
             pltpu.VMEM((ROT * 4 * TALL, 128), jnp.float32),
             pltpu.VMEM((TALL, 128), jnp.float32),
             pltpu.VMEM((GROUPS, CAP * PIECE, PIECE), jnp.bfloat16),
             pltpu.VMEM((4, 128), jnp.float32),
             dma((4,)),
+            dma((1,)),
+            dma((3,)),
             dma((2,)),
-            dma((3,)),
+            dma((2,)),
             dma((CHUNKS,)),
             dma((CHUNKS,)),
             dma((CHUNKS,)),
@@ -479,6 +521,17 @@
         pltpu.with_memory_space_constraint(x, pltpu.HBM)
         for x in (embeddings, frame_weight.reshape(4, 128), candidates.reshape(4, count), owner)
     ))
+    out, best = pl.pallas_call(
+        settle,
+        out_shape=(
+            jax.ShapeDtypeStruct(out.shape, out.dtype),
+            jax.ShapeDtypeStruct(best.shape, best.dtype),
+        ),
+        in_specs=[vmem, vmem],
+        out_specs=(hbm, hbm),
+        scratch_shapes=[dma((2,))],
+        name="settle",
+    )(*(pltpu.with_memory_space_constraint(x, pltpu.VMEM) for x in (out, best)))
     return best.reshape(F), out.reshape(1, 1, GROUPS, CAP, PIECE, PIECE)
 
 

time: 46.9 us -> 43.1 us (0.919)
  Pallas kernels: 44.8 us -> 42.2 us
  local copies, waits for them, and re-layouts: 1.37 us -> 0 us
    pallas_call x1, Pallas kernels: 44.8 us -> 41.4 us  [body(): pl.pallas_call(functools.partial(kernel, n_blk), out_shape=(jax.ShapeDtyp...]
    unnamed x2 -> x0, local copies, waits for them, and re-layouts: 1.37 us -> none
    pallas_call x0 -> x1, Pallas kernels: none -> 0.81 us  [body(): pl.pallas_call(settle, out_shape=(jax.ShapeDtypeStruct(out.shape, out.dty...]
where the time goes in v3:
time: 43.1 us; the launch traced here: 42.9 us
  Pallas kernels  42.2 us (98%)
  between operations  0.64 us (1%)
    pallas_call x1, Pallas kernels, body(): pl.pallas_call(functools.partial(kernel, n_blk), out_shape=(jax.ShapeDtyp...  41.4 us

profile of v3, /device:TPU:2, one launch (start us, length us, event | category | flops | bytes accessed | tf_op | source)
XLA Modules:
  0.0 42.9 jit_solution(524820079516264781)
XLA Ops:
  0.6 41.4 %window_join.1 = (bf16[8,256,128]{2,1,0:T(8,128)(2,1)S(1)}, f32[4,128]{1,0:T(4,128)S(1)}) custom-call(bf16[512,512]{1,0:T(8,128)(2,1)} %emb.1, bf16[4,128]{1,0:T(4,128)(2,1)} %bitcast.5, s32[4,8]{1,0:T(4,128)} %bitcast.4, s32[512]{0:T(512)} %owner_in.1), custom_call_target="tpu_custom_call" | custom-call | tf_op jit(solution)/shard_map/window_join/pallas_call | solution.py:475
  42.1 0.8 %settle.1 = (bf16[8,256,128]{2,1,0:T(8,128)(2,1)}, f32[4,128]{1,0:T(4,128)}) custom-call(bf16[8,256,128]{2,1,0:T(8,128)(2,1)S(1)} %get-tuple-element.6.out_in, f32[4,128]{1,0:T(4,128)S(1)} %get-tuple-element.7.best_in), custom_call_target="tpu_custom_call" | custom-call | tf_op jit(solution)/shard_map/settle/pallas_call | solution.py:524

commit v4 on v3

--- a/solution.py
+++ b/solution.py
@@ -157,7 +157,6 @@
         )
 
     barrier = pltpu.get_barrier_semaphore()
-    order = [(0, 1), (2, 1), (1, 1), (3, 1), (2, 0), (1, 0), (3, 0)]
     per_row = n_blk // 4
     turn = 1 - 2 * lax.rem(g, 2)
     y_lo = b // per_row
@@ -182,27 +181,15 @@
     greet((b, peer(1, 0)))
     greet((b, peer(3, 0)))
     greet(y_up)
+    own_weights = pltpu.make_async_copy(w_in, w_own, loc.at[2])
+    own_weights.start()
 
     own_rows = pltpu.make_async_copy(emb, rows, loc.at[0])
     own_cols = pltpu.make_async_copy(emb, cols.at[1], loc.at[0])
     own_list = pltpu.make_async_copy(cand, listing, loc.at[1])
-    own_weights = pltpu.make_async_copy(w_in, w_own, loc.at[2])
     owners = pltpu.make_async_copy(owner_in, owner, loc.at[3])
-    own_weights.start()
-
-    @pl.when(even)
-    def _():
-        own_cols.start()
-
-    @pl.when(odd)
-    def _():
-        own_rows.start()
-        own_list.start()
-
-    owners.start()
+
     own_slot = 2 * (1 - core)
-    own_weights.wait()
-    wx[own_slot, 0:4, :] = w_own[...].astype(jnp.float32)
     pl.semaphore_wait(barrier, 6)
 
     quarter = F // CHUNKS
@@ -252,23 +239,57 @@
     @pl.when(even)
     def _():
         greet(behind(2), flood.at[6])
+        to_odd.start()
+
+    @pl.when(odd)
+    def _():
+        ahead[0].start()
+        to_even.start()
+
+    greet((b, peer(3, 0)), flood.at[0])
+
+    @pl.when(even)
+    def _():
+        own_cols.start()
+
+    @pl.when(odd)
+    def _():
+        own_rows.start()
+        own_list.start()
+
+    owners.start()
+    own_weights.wait()
+    wx[own_slot, 0:4, :] = w_own[...].astype(jnp.float32)
+
+    @pl.when(even)
+    def _():
         for copy in w_even[1:]:
             copy.start()
-        to_odd.start()
 
     @pl.when(odd)
     def _():
         for copy in w_odd:
             copy.start()
-        to_even.start()
-        for copy in ahead:
+        for copy in ahead[1:]:
             copy.start()
 
-    greet((b, peer(3, 0)), flood.at[0])
     pl.when(even & jnp.logical_not(first))(send_rows)
-    for k in range(4):
+
+    def pass_on(k):
         hear(k)
         greet(y_down, flood.at[k + 1])
+
+    pass_on(0)
+    pass_on(1)
+    to_even.wait_recv()
+
+    @pl.when(odd)
+    def _():
+        ahead[CHUNKS - 2].wait_send()
+        relay.start()
+
+    pass_on(2)
+    pass_on(3)
 
     def tell_behind():
         hear(4)
@@ -278,13 +299,6 @@
     def _():
         send_rows()
         tell_behind()
-
-    to_even.wait_recv()
-
-    @pl.when(odd)
-    def _():
-        ahead[CHUNKS - 2].wait_send()
-        relay.start()
 
     s_ref[:, :, 0:PAD, :] = jnp.zeros((ROT, 4, PAD, 128), jnp.float32)
     s_ref[:, :, PAD + F :, :] = jnp.zeros((ROT, 4, s_ref.shape[2] - PAD - F, 128), jnp.float32)
@@ -308,8 +322,11 @@
     weight(1, 1, 3).wait_recv()
     owners.wait()
     row_weights(wx, a_ref)
-    for t in range(ROT):
+    def columns(t, carry):
         column_weights(wx, t + 1, acs_ref.at[t])
+        return carry
+
+    lax.fori_loop(0, ROT, columns, 0)
 
     count = listing.shape[1]
     where, slot_of, start_of = [], [], []
@@ -322,15 +339,17 @@
         for m in range(n):
             slot = slot + jnp.where(where[m] == where[n], 1, 0)
         slot_of.append(slot)
-    for d in range(GROUPS):
-        for s in range(CAP):
-            start, there = jnp.int32(0), jnp.int32(0)
-            for n in range(count):
-                here = (where[n] == d) & (slot_of[n] == s)
-                start = jnp.where(here, start_of[n], start)
-                there = jnp.where(here, 1, there)
-            plan[0, d * CAP + s] = start
-            plan[1, d * CAP + s] = there
+    def planned(k, carry):
+        start, there = jnp.int32(0), jnp.int32(0)
+        for n in range(count):
+            here = where[n] * CAP + slot_of[n] == k
+            start = jnp.where(here, start_of[n], start)
+            there = jnp.where(here, 1, there)
+        plan[0, k] = start
+        plan[1, k] = there
+        return carry
+
+    lax.fori_loop(0, GROUPS * CAP, planned, 0)
 
     def half_tile(k, carry):
         h = jnp.where(first, jnp.where(k < 4, k // 2, k - 4), k // 3)
@@ -389,25 +408,35 @@
     def piece_copy(d):
         return remote(bucket.at[d], out.at[g], p_send.at[d], p_recv.at[g], (home, d))
 
+    def nth(k):
+        j = lax.rem(k + k // 4, 4)
+        return peer(lax.rem(j, 2) * 2 + j // 2, 1 - k // 4)
+
+    own_piece = pltpu.make_async_copy(bucket.at[g], out.at[g], loc.at[0])
+
+    def send_pieces(k, carry):
+        d = nth(k)
+        fill(d)
+
+        @pl.when((k < GROUPS - 1) | even)
+        def _():
+            piece_copy(d).start()
+
+        @pl.when((k == GROUPS - 1) & odd)
+        def _():
+            own_piece.start()
+
+        return carry
+
     pl.when(odd & last)(functools.partial(hear, 7))
-    for dx, dy in order:
-        d = peer(dx, dy)
-        fill(d)
-        piece_copy(d).start()
-    fill(g)
-    own_piece = pltpu.make_async_copy(bucket.at[g], out.at[g], loc.at[0])
-
-    @pl.when(even)
-    def _():
-        piece_copy(g).start()
-
-    @pl.when(odd)
-    def _():
-        own_piece.start()
-
-    for r in range(4):
-        block = jnp.transpose(m_ref[PAD + 128 * r : PAD + 128 * (r + 1), :])
-        top[r : r + 1, :] = jnp.max(block, axis=0, keepdims=True) * SCALE
+    lax.fori_loop(0, GROUPS, send_pieces, 0)
+
+    def best_of(r, carry):
+        block = jnp.transpose(m_ref[pl.ds(PAD + 128 * r, 128), :])
+        top[pl.ds(r, 1), :] = jnp.max(block, axis=0, keepdims=True) * SCALE
+        return carry
+
+    lax.fori_loop(0, 4, best_of, 0)
     top_home = remote(top, best, b_sem.at[0], b_sem.at[1], behind(2))
     top_here = pltpu.make_async_copy(top, best, loc.at[1])
 
@@ -419,8 +448,11 @@
     def _():
         top_here.start()
 
-    for dx, dy in order:
-        piece_copy(peer(dx, dy)).wait_send()
+    def sent(k, carry):
+        piece_copy(nth(k)).wait_send()
+        return carry
+
+    lax.fori_loop(0, GROUPS - 1, sent, 0)
 
     @pl.when(even & last)
     def _():
@@ -452,9 +484,12 @@
         top_here.wait()
         own_piece.wait()
 
-    for dx, dy in order:
-        d = peer(dx, dy)
+    def received(k, carry):
+        d = nth(k)
         remote(bucket.at[d], out.at[d], p_send.at[d], p_recv.at[d], (home, d)).wait_recv()
+        return carry
+
+    lax.fori_loop(0, GROUPS - 1, received, 0)
 
 
 def settle(out_in, best_in, out, best, sems):

time: 43.1 us -> 43.2 us (level)
  the two profiles are of different devices: /device:TPU:2 before, /device:TPU:32 now
where the time goes in v4:
time: 43.2 us; the launch traced here: 43.1 us
  Pallas kernels  42.5 us (98%)
  between operations  0.64 us (1%)
    pallas_call x1, Pallas kernels, body(): pl.pallas_call(functools.partial(kernel, n_blk), out_shape=(jax.ShapeDtyp...  41.6 us

profile of v4, /device:TPU:32, one launch (start us, length us, event | category | flops | bytes accessed | tf_op | source)
XLA Modules:
  0.0 43.1 jit_solution(10943634339824840441)
XLA Ops:
  0.6 41.6 %window_join.1 = (bf16[8,256,128]{2,1,0:T(8,128)(2,1)S(1)}, f32[4,128]{1,0:T(4,128)S(1)}) custom-call(bf16[512,512]{1,0:T(8,128)(2,1)} %emb.1, bf16[4,128]{1,0:T(4,128)(2,1)} %bitcast.5, s32[4,8]{1,0:T(4,128)} %bitcast.4, s32[512]{0:T(512)} %owner_in.1), custom_call_target="tpu_custom_call" | custom-call | tf_op jit(solution)/shard_map/window_join/pallas_call | solution.py:510
  42.3 0.8 %settle.1 = (bf16[8,256,128]{2,1,0:T(8,128)(2,1)}, f32[4,128]{1,0:T(4,128)}) custom-call(bf16[8,256,128]{2,1,0:T(8,128)(2,1)S(1)} %get-tuple-element.6.out_in, f32[4,128]{1,0:T(4,128)S(1)} %get-tuple-element.7.best_in), custom_call_target="tpu_custom_call" | custom-call | tf_op jit(solution)/shard_map/settle/pallas_call | solution.py:559

commit v5 on v3

--- a/solution.py
+++ b/solution.py
@@ -133,6 +133,7 @@
     f_send,
     f_recv,
     y_send,
+    y_recv,
     w_send,
     w_recv,
     c_sem,
@@ -227,7 +228,10 @@
         remote(chunk(cols.at[2], k), chunk(cols.at[1], k), f_send.at[k], f_recv.at[k], behind(1))
         for k in range(CHUNKS)
     ]
-    relay = remote(cols.at[0], cols.at[2], y_send.at[0], e_recv.at[2], behind(2))
+    relay = [
+        remote(chunk(cols.at[0], k), chunk(cols.at[2], k), y_send.at[k], y_recv.at[k], behind(2))
+        for k in range(CHUNKS)
+    ]
 
     def weight(k, steps, slot):
         return remote(wx.at[own_slot], wx.at[slot], w_send.at[k], w_recv.at[slot], behind(steps))
@@ -284,7 +288,8 @@
     @pl.when(odd)
     def _():
         ahead[CHUNKS - 2].wait_send()
-        relay.start()
+        for copy in relay:
+            copy.start()
 
     s_ref[:, :, 0:PAD, :] = jnp.zeros((ROT, 4, PAD, 128), jnp.float32)
     s_ref[:, :, PAD + F :, :] = jnp.zeros((ROT, 4, s_ref.shape[2] - PAD - F, 128), jnp.float32)
@@ -365,7 +370,8 @@
         @pl.when(t == 2)
         def _():
             hear(4)
-            relay.wait_recv()
+            for copy in relay:
+                copy.wait_recv()
 
         product(rows, cols, t, s_ref, 0, F)
         smooth(s_ref, a_ref, acs_ref, t_ref, m_ref, t, 0, STEP)
@@ -448,7 +454,8 @@
             if k != CHUNKS - 2:
                 ahead[k].wait_send()
         to_even.wait_send()
-        relay.wait_send()
+        for copy in relay:
+            copy.wait_send()
         top_here.wait()
         own_piece.wait()
 
@@ -505,7 +512,8 @@
             dma((CHUNKS,)),
             dma((CHUNKS,)),
             dma((CHUNKS,)),
-            dma((1,)),
+            dma((CHUNKS,)),
+            dma((CHUNKS,)),
             dma((3,)),
             dma((4,)),
             dma((2,)),

time: 43.1 us -> 43.1 us (level)
  the two profiles are of different devices: /device:TPU:2 before, /device:TPU:14 now
where the time goes in v5:
time: 43.1 us; the launch traced here: 43 us
  Pallas kernels  42.4 us (98%)
  between operations  0.64 us (1%)
    pallas_call x1, Pallas kernels, body(): pl.pallas_call(functools.partial(kernel, n_blk), out_shape=(jax.ShapeDtyp...  41.5 us

profile of v5, /device:TPU:14, one launch (start us, length us, event | category | flops | bytes accessed | tf_op | source)
XLA Modules:
  0.0 43.0 jit_solution(647398521062702034)
XLA Ops:
  0.6 41.5 %window_join.1 = (bf16[8,256,128]{2,1,0:T(8,128)(2,1)S(1)}, f32[4,128]{1,0:T(4,128)S(1)}) custom-call(bf16[512,512]{1,0:T(8,128)(2,1)} %emb.1, bf16[4,128]{1,0:T(4,128)(2,1)} %bitcast.5, s32[4,8]{1,0:T(4,128)} %bitcast.4, s32[512]{0:T(512)} %owner_in.1), custom_call_target="tpu_custom_call" | custom-call | tf_op jit(solution)/shard_map/window_join/pallas_call | solution.py:482
  42.2 0.8 %settle.1 = (bf16[8,256,128]{2,1,0:T(8,128)(2,1)}, f32[4,128]{1,0:T(4,128)}) custom-call(bf16[8,256,128]{2,1,0:T(8,128)(2,1)S(1)} %get-tuple-element.6.out_in, f32[4,128]{1,0:T(4,128)S(1)} %get-tuple-element.7.best_in), custom_call_target="tpu_custom_call" | custom-call | tf_op jit(solution)/shard_map/settle/pallas_call | solution.py:532

commit v6 on v5

--- a/solution.py
+++ b/solution.py
@@ -338,8 +338,8 @@
             plan[1, d * CAP + s] = there
 
     def half_tile(k, carry):
-        h = jnp.where(first, jnp.where(k < 4, k // 2, k - 4), k // 3)
-        t = jnp.where(first, jnp.where(k < 4, lax.rem(k, 2), 2), lax.rem(k, 3))
+        h = k // 3
+        t = lax.rem(k, 3)
 
         @pl.when((t == 0) & (h == 0))
         def _():
@@ -355,19 +355,31 @@
                 ahead[c].wait_recv()
                 passed[c].start()
 
-        pl.when((k == 2) & jnp.logical_not(first))(tell_behind)
+        pl.when(k == 2)(tell_behind)
         pl.when(k == 4)(functools.partial(hear, 5))
         product(rows, cols, t, s_ref, h * half, half)
         smooth(s_ref, a_ref, acs_ref, t_ref, m_ref, t, h * (F - 8 * HALF_STEP + 12) - 12, HALF_STEP)
         return carry
 
     def tile(t, carry):
-        @pl.when(t == 1)
+        @pl.when(even & (t == 0))
+        def _():
+            for copy in to_rows:
+                copy.wait_recv()
+
+        @pl.when(even & (t == 2))
+        def _():
+            hear(5)
+            for c in range(CHUNKS):
+                ahead[c].wait_recv()
+                passed[c].start()
+
+        @pl.when(odd & (t == 1))
         def _():
             for c in range(CHUNKS):
                 passed[c].wait_recv()
 
-        @pl.when(t == 2)
+        @pl.when(odd & (t == 2))
         def _():
             hear(4)
             for copy in relay:
@@ -377,11 +389,11 @@
         smooth(s_ref, a_ref, acs_ref, t_ref, m_ref, t, 0, STEP)
         return carry
 
-    @pl.when(even)
+    @pl.when(even & jnp.logical_not(first))
     def _():
         lax.fori_loop(0, 2 * ROT, half_tile, 0)
 
-    @pl.when(odd)
+    @pl.when(odd | first)
     def _():
         lax.fori_loop(0, ROT, tile, 0)
 

time: 43.1 us -> 43.1 us (level)
  the two profiles are of different devices: /device:TPU:14 before, /device:TPU:2 now
where the time goes in v6:
time: 43.1 us; the launch traced here: 42.9 us
  Pallas kernels  42.3 us (98%)
  between operations  0.64 us (1%)
    pallas_call x1, Pallas kernels, body(): pl.pallas_call(functools.partial(kernel, n_blk), out_shape=(jax.ShapeDtyp...  41.5 us

profile of v6, /device:TPU:2, one launch (start us, length us, event | category | flops | bytes accessed | tf_op | source)
XLA Modules:
  0.0 42.9 jit_solution(10483693864059211858)
XLA Ops:
  0.6 41.5 %window_join.1 = (bf16[8,256,128]{2,1,0:T(8,128)(2,1)S(1)}, f32[4,128]{1,0:T(4,128)S(1)}) custom-call(bf16[512,512]{1,0:T(8,128)(2,1)} %emb.1, bf16[4,128]{1,0:T(4,128)(2,1)} %bitcast.5, s32[4,8]{1,0:T(4,128)} %bitcast.4, s32[512]{0:T(512)} %owner_in.1), custom_call_target="tpu_custom_call" | custom-call | tf_op jit(solution)/shard_map/window_join/pallas_call | solution.py:494
  42.1 0.8 %settle.1 = (bf16[8,256,128]{2,1,0:T(8,128)(2,1)}, f32[4,128]{1,0:T(4,128)}) custom-call(bf16[8,256,128]{2,1,0:T(8,128)(2,1)S(1)} %get-tuple-element.6.out_in, f32[4,128]{1,0:T(4,128)S(1)} %get-tuple-element.7.best_in), custom_call_target="tpu_custom_call" | custom-call | tf_op jit(solution)/shard_map/settle/pallas_call | solution.py:544
